TPU v7x, 32 devices: a whole 2x2x4 slice. The times are simulated.
32 devices in a mesh: outer: 4 (over y, x), inner: 8 (over z, core).
Axes of the slice: x: 2, y: 2, z: 4, core: 2. Of those that a mesh axis runs over, the one named last changes fastest.
Arguments:
- tokens: bfloat16 [512, 8192], P(None, 'outer'), may hold values from -60 to 60
- base_gate: bfloat16 [8192, 28672], P('outer', 'inner'), may hold values from -0.06629126 to 0.06629126
- base_up: bfloat16 [8192, 28672], P('outer', 'inner'), may hold values from -0.06629126 to 0.06629126
- adjusted_gate: bfloat16 [8192, 28672], P('outer', 'inner'), may hold values from -0.092807765 to 0.092807765
- adjusted_up: bfloat16 [8192, 28672], P('outer', 'inner'), may hold values from -0.092807765 to 0.092807765
- slab_block: int32 [8], replicated, may hold values from 0 to 7, each once
Outputs:
- correlation: float32 [3584, 28672], P('outer', 'inner')
Inputs may be any that keep to these rules, and one draw needn't show every extreme that they name: `slab_block`: each block number appears once.
All inputs are finite; a program needn't handle non-finite values.
Results may differ from a plain program's by a relative error of at most 0.004.
Values may be sent and summed in bfloat16 or wider, within the bound.
A program may use at most 192 MiB of HBM per device.

v0:
```python
import jax
import jax.numpy as jnp
from jax import lax
from jax.sharding import PartitionSpec as P


def spread(value, axis, source):
    kept = jnp.where(lax.axis_index(axis) == source, value, 0).astype(value.dtype)
    return lax.psum(kept, axis)


def local(tokens, base_gate, base_up, adjusted_gate, adjusted_up, slab_block):
    units = base_gate.shape[1]
    total_tokens = tokens.shape[0]
    outer_count = lax.axis_size("outer")
    parts = [
        jnp.dot(tokens, weight, preferred_element_type=jnp.float32)
        for weight in (base_gate, base_up, adjusted_gate, adjusted_up)
    ]
    terms = lax.psum_scatter(
        jnp.concatenate(parts, axis=1), "outer", scatter_dimension=0, tiled=True
    )
    hidden_base = jax.nn.silu(terms[:, :units]) * terms[:, units : 2 * units]
    hidden_adjusted = jax.nn.silu(terms[:, 2 * units : 3 * units]) * terms[:, 3 * units :]
    hidden = jnp.concatenate([hidden_base, hidden_adjusted], axis=1)
    sums = lax.psum(jnp.sum(hidden, axis=0, keepdims=True), "outer")
    mean = sums / total_tokens
    centered = hidden - mean
    squares = lax.psum(jnp.sum(centered * centered, axis=0, keepdims=True), "outer")
    var = squares / total_tokens
    standard = (centered * lax.rsqrt(var + 1e-05)).astype(jnp.bfloat16)
    base_scores = standard[:, :units]
    adjusted_scores = standard[:, units:]
    slab = spread(base_scores, "inner", slab_block[0])
    contract = (((0,), (0,)), ((), ()))
    full_slab, full_adjusted = (
        lax.all_gather(slab, "outer", axis=0, tiled=True),
        lax.all_gather(adjusted_scores, "outer", axis=0, tiled=True),
    )
    row_count = units // outer_count
    own_rows = lax.dynamic_slice_in_dim(
        full_slab, lax.axis_index("outer") * row_count, row_count, 1
    )
    gram = lax.dot_general(own_rows, full_adjusted, contract, preferred_element_type=jnp.float32)
    return gram / total_tokens


def solution(mesh):
    return jax.shard_map(
        local,
        mesh=mesh,
        in_specs=(
            P(None, "outer"),
            P("outer", "inner"),
            P("outer", "inner"),
            P("outer", "inner"),
            P("outer", "inner"),
            P(),
        ),
        out_specs=P("outer", "inner"),
        check_vma=False,
    )
```

profile of v0, /device:TPU:0, one launch (start us, length us, event | category | flops | bytes accessed | tf_op | source)
XLA Modules:
  0.0 549.3 jit_solution(2040453812901652797)
XLA Ops:
  6.5 1.6 copy-done
  8.1 13.0 %fusion.3 = f32[512,3584]{1,0:T(8,128)} fusion(bf16[512,2048]{1,0:T(8,128)(2,1)S(1)} %copy-done, bf16[2048,3584]{1,0:T(8,128)(2,1)} %param.7), kind=kOutput, calls=%fused_computation.13 | convolution fusion | flops 7516192768 | bytes 24117248 | tf_op jit(solution)/shard_map/dot_general | solution.py:17
  21.1 9.9 %fusion.4 = f32[512,3584]{1,0:T(8,128)} fusion(bf16[512,2048]{1,0:T(8,128)(2,1)S(1)} %copy-done, bf16[2048,3584]{1,0:T(8,128)(2,1)S(1)} %copy-done.3), kind=kOutput, calls=%fused_computation.14 | convolution fusion | flops 7516192768 | bytes 24117248 | tf_op jit(solution)/shard_map/dot_general | solution.py:17
  31.0 13.0 %fusion.5 = f32[512,3584]{1,0:T(8,128)} fusion(bf16[512,2048]{1,0:T(8,128)(2,1)S(1)} %copy-done, bf16[2048,3584]{1,0:T(8,128)(2,1)} %param.9), kind=kOutput, calls=%fused_computation.15 | convolution fusion | flops 7516192768 | bytes 24117248 | tf_op jit(solution)/shard_map/dot_general | solution.py:17
  44.0 9.8 %fusion.6 = f32[512,3584]{1,0:T(8,128)} fusion(bf16[512,2048]{1,0:T(8,128)(2,1)S(1)} %copy-done, bf16[2048,3584]{1,0:T(8,128)(2,1)S(1)} %bitcast.21), kind=kOutput, calls=%fused_computation.16 | convolution fusion | flops 7516192768 | bytes 24117248 | tf_op jit(solution)/shard_map/dot_general | solution.py:17
  53.8 20.5 %pad_maximum_fusion = f32[512,14336]{1,0:T(8,128)} fusion(f32[512,3584]{1,0:T(8,128)} %fusion.6, f32[512,3584]{1,0:T(8,128)} %fusion.5, f32[512,3584]{1,0:T(8,128)} %fusion.4, f32[512,3584]{1,0:T(8,128)} %fusion.3), kind=kLoop, calls=%fused_computation | loop fusion | flops 22020096 | bytes 58720256 | tf_op jit(solution)/shard_map/concatenate | solution.py:21
  74.4 0.2 all-reduce.2.cloned.1.call-start
  74.6 0.4 copy-done.4
  75.0 258.1 %reduce-scatter.2.cloned.1.call-done = f32[128,14336]{1,0:T(8,128)} async-done(((f32[512,14336]{1,0:T(8,128)}), f32[128,14336]{1,0:T(8,128)}) %reduce-scatter.2.cloned.1.call-update) | async-done | bytes 7340048 | tf_op jit(solution)/shard_map/reduce_scatter | solution.py:20
  333.1 4.1 slice_multiply_fusion.1
  337.2 1.2 copy-done.2
  338.4 0.2 fusion
  338.7 15.4 %psum.21 = f32[1,7168]{1,0:T(1,128)S(1)} all-reduce(f32[1,7168]{1,0:T(1,128)S(1)} %bitcast.19), channel_id=1, replica_groups=mesh['outer'=4,'inner'=8] {'outer'}, use_global_device_ids=true, to_apply=%region_2.3 | all-reduce | flops 7168 | bytes 57344 | tf_op jit(solution)/shard_map/psum | solution.py:26
  354.1 1.9 multiply_reduce_fusion
  356.0 15.1 %psum.22 = f32[1,7168]{1,0:T(1,128)S(1)} all-reduce(f32[1,7168]{1,0:T(1,128)S(1)} %bitcast.17), channel_id=1, replica_groups=mesh['outer'=4,'inner'=8] {'outer'}, use_global_device_ids=true, to_apply=%region_4.5 | all-reduce | flops 7168 | bytes 57344 | tf_op jit(solution)/shard_map/psum | solution.py:29
  371.2 1.9 multiply_convert_fusion
  373.1 1.4 slice_select_fusion
  374.5 0.0 all-gather.5.cloned.1.call-start
  374.6 0.7 all-gather.5.cloned.1.call-update
  375.3 0.0 all-gather.3.cloned.1.call-start
  375.3 57.3 %all-reduce.2.cloned.1.call-done = bf16[128,3584]{1,0:T(8,128)(2,1)} async-done(((bf16[128,3584]{1,0:T(8,128)(2,1)}), bf16[128,3584]{1,0:T(8,128)(2,1)}) %all-reduce.2.cloned.1.call-update) | async-done | bytes 917520 | tf_op jit(solution)/shard_map/psum | solution.py:9
  432.7 49.1 %all-gather.5.cloned.1.call-done = bf16[512,3584]{1,0:T(8,128)(2,1)} async-done(((bf16[128,3584]{1,0:T(8,128)(2,1)}), bf16[512,3584]{1,0:T(8,128)(2,1)}) %all-gather.5.cloned.1.call-update) | async-done | bytes 3670032 | tf_op jit(solution)/shard_map/all_gather | solution.py:38
  481.8 50.1 %all-gather.3.cloned.1.call-done = bf16[512,3584]{1,0:T(8,128)(2,1)} async-done(((bf16[128,3584]{1,0:T(8,128)(2,1)}), bf16[512,3584]{1,0:T(8,128)(2,1)}) %all-gather.3.cloned.1.call-update) | async-done | bytes 3670032 | tf_op jit(solution)/shard_map/all_gather | solution.py:37
  531.9 10.9 %convolution_multiply_fusion = f32[896,3584]{1,0:T(8,128)} fusion(bf16[512,3584]{1,0:T(8,128)(2,1)} %all-gather.5.cloned.1.call-done, bf16[512,3584]{1,0:T(8,128)(2,1)} %all-gather.3.cloned.1.call-done, s32[]{:T(128)S(6)} %select_n.13), kind=kOutput, calls=%fused_computation.1 | convolution fusion | flops 3291545600 | bytes 17432580 | tf_op jit(solution)/shard_map/dot_general | solution.py:44
  (22 shorter events, 0.2 us)
Async XLA Ops:
  6.5 1.6 copy-start
  6.5 326.6 %reduce-scatter.2.cloned.1.call-start = ((), (), s32[]{:S(2)}) async-start(), calls=%async_computation.1 | async-start | bytes 36700160 | tf_op jit(solution)/shard_map/reduce_scatter | solution.py:20
  8.1 13.0 %copy-start.3 = (bf16[2048,3584]{1,0:T(8,128)(2,1)S(1)}, bf16[2048,3584]{1,0:T(8,128)(2,1)}, u32[]{:S(2)}) copy-start(bf16[2048,3584]{1,0:T(8,128)(2,1)} %param.8) | copy-start | bytes 44040196
  21.1 22.9 %slice-start = ((s8[14680064]{0:T(1024)(128)(4,1)}), s8[2097152]{0:T(1024)(128)(4,1)S(1)}, s32[]{:S(2)}) async-start(s8[14680064]{0:T(1024)(128)(4,1)} %bitcast.20), calls=%async_computation.5 | async-start | bytes 4194304
  21.1 22.9 %slice-start.1 = ((s8[14680064]{0:T(1024)(128)(4,1)}), s8[4194304]{0:T(1024)(128)(4,1)S(1)}, s32[]{:S(2)}) async-start(s8[14680064]{0:T(1024)(128)(4,1)} %bitcast.20), calls=%async_computation.6 | async-start | bytes 8388608
  31.0 13.0 %slice-start.2 = ((s8[14680064]{0:T(1024)(128)(4,1)}), s8[4194304]{0:T(1024)(128)(4,1)S(1)}, s32[]{:S(2)}) async-start(s8[14680064]{0:T(1024)(128)(4,1)} %bitcast.20), calls=%async_computation.7 | async-start | bytes 8388608
  31.0 13.0 %slice-start.3 = ((s8[14680064]{0:T(1024)(128)(4,1)}), s8[4194304]{0:T(1024)(128)(4,1)S(1)}, s32[]{:S(2)}) async-start(s8[14680064]{0:T(1024)(128)(4,1)} %bitcast.20), calls=%async_computation.8 | async-start | bytes 8388608
  74.3 0.7 copy-start.4
  74.4 358.3 %all-reduce.2.cloned.1.call-start = ((), (), s32[]{:S(2)}) async-start(), calls=%async_computation.2 | async-start | bytes 1835008 | tf_op jit(solution)/shard_map/psum | solution.py:9
  337.2 1.2 copy-start.2
  374.5 107.2 %all-gather.5.cloned.1.call-start = ((), (), s32[]{:S(2)}) async-start(), calls=%async_computation.4 | async-start | bytes 4587520 | tf_op jit(solution)/shard_map/all_gather | solution.py:38
  375.3 156.6 %all-gather.3.cloned.1.call-start = ((), (), s32[]{:S(2)}) async-start(), calls=%async_computation.3 | async-start | bytes 4587520 | tf_op jit(solution)/shard_map/all_gather | solution.py:37
  531.9 10.9 %copy-start.1 = (bf16[512,2048]{1,0:T(8,128)(2,1)S(1)}, bf16[512,2048]{1,0:T(8,128)(2,1)}, u32[]{:S(2)}) copy-start(bf16[512,2048]{1,0:T(8,128)(2,1)} %param.6) | copy-start | bytes 6291460
Sparse Core Ops, SparseCore 0:
  74.5 258.5 reduce-scatter.1
  374.7 57.9 all-reduce.1
  434.5 47.2 all-gather.4
  483.5 48.3 all-gather.2
where the time goes:
time: 550 us; the launch traced here: 549 us
  waiting for transfers between devices  415 us (75%)
  matrix products  56.5 us (10%)
  blocking collectives  30.5 us (6%)
  other arithmetic  30.2 us (5%)
  between operations  13.3 us (2%)
    reduce_scatter x1, waiting for transfers between devices, local(): lax.psum_scatter(jnp.concatenate(parts, axis=1), 'outer', scatter_dimensi...  258 us
    psum x1, waiting for transfers between devices, spread(): return lax.psum(kept, axis)  57.3 us
    all_gather x1, waiting for transfers between devices, local(): lax.all_gather(slab, 'outer', axis=0, tiled=True)  50.1 us
    all_gather x1, waiting for transfers between devices, local(): lax.all_gather(adjusted_scores, 'outer', axis=0, tiled=True)  49.1 us
    dot_general x4, matrix products, local(): jnp.dot(tokens, weight, preferred_element_type=jnp.float32)  45.6 us
    concatenate x1, other arithmetic, local(): jnp.concatenate(parts, axis=1)  20.5 us
    psum x1, blocking collectives, local(): sums = lax.psum(jnp.sum(hidden, axis=0, keepdims=True), 'outer')  15.4 us
    psum x1, blocking collectives, local(): lax.psum(jnp.sum(centered * centered, axis=0, keepdims=True), 'outer')  15.1 us
  transfers between devices with their start and end apart: 4, of which 4 were waited for; matrix products, arithmetic and copies ran while one was open for 0% of the time, Pallas kernels for 0%

commit v1 on v0

v1 whole, which is shorter than its diff:
```python
import jax
import jax.numpy as jnp
from jax import lax
from jax.sharding import PartitionSpec as P

WIRE = jnp.float16


def swap(value, axis, bit):
    size = lax.axis_size(axis)
    return lax.ppermute(value, axis, [(i, i ^ bit) for i in range(size)])


def bits_of(size):
    bits = []
    while (1 << len(bits)) < size:
        bits.append(1 << len(bits))
    return bits


def halve(block, axis, bits):
    size = lax.axis_size(axis)
    me = lax.axis_index(axis)
    held = {m: block(me ^ m) for m in range(size)}
    live = list(range(size))
    for bit in bits:
        keep = [m for m in live if not m & bit]
        got = {m: swap(held[m ^ bit].astype(WIRE), axis, bit) for m in reversed(keep)}
        held = {m: held[m].astype(jnp.float32) + got[m].astype(jnp.float32) for m in keep}
        live = keep
    return held[0]


def double(value, axis, bits):
    held = {0: value}
    for bit in bits:
        held.update({m ^ bit: swap(v, axis, bit) for m, v in list(held.items())})
    return held


def scores(gate, up):
    hidden = jax.nn.silu(gate) * up
    mean = jnp.mean(hidden, axis=0, keepdims=True)
    centered = hidden - mean
    var = jnp.mean(centered * centered, axis=0, keepdims=True)
    return (centered * lax.rsqrt(var + 1e-05)).astype(jnp.bfloat16)


def local(tokens, base_gate, base_up, adjusted_gate, adjusted_up, slab_block):
    units = base_gate.shape[1]
    total_tokens = tokens.shape[0]
    outer_count = lax.axis_size("outer")
    inner_count = lax.axis_size("inner")
    outer = lax.axis_index("outer")
    inner = lax.axis_index("inner")
    width = units // outer_count
    bits = bits_of(outer_count)
    back = bits[::-1]

    def term(weight):
        def block(b):
            part = lax.dynamic_slice_in_dim(weight, b * width, width, 1)
            return jnp.dot(tokens, part, preferred_element_type=jnp.float32).astype(WIRE)
        return block

    def multiply(gate, up):
        return tuple(
            jnp.dot(tokens, w, preferred_element_type=jnp.float32).astype(WIRE)
            for w in (gate, up)
        )

    def nothing(gate, up):
        return tuple(jnp.zeros((total_tokens, units), WIRE) for _ in range(2))

    slab_gate, slab_up = lax.cond(
        inner == slab_block[0], multiply, nothing, base_gate, base_up
    )
    core = inner % 2
    mine = jnp.where(core == 0, slab_gate, slab_up)
    other = jnp.where(core == 0, slab_up, slab_gate)
    mine = mine + swap(other, "inner", 1)

    def slab_term(b):
        return lax.dynamic_slice_in_dim(mine, b * width, width, 1)

    half = total_tokens // 2
    slab_sum = jnp.concatenate(
        [
            halve(lambda b: slab_term(b)[:half], "outer", bits),
            halve(lambda b: slab_term(b)[half:], "outer", back),
        ],
        axis=0,
    )
    across = swap(slab_sum, "inner", 1)
    slab = scores(
        jnp.where(core == 0, slab_sum, across), jnp.where(core == 0, across, slab_sum)
    )
    here = (inner // 2) == (slab_block[0] // 2)
    part = lax.dynamic_slice_in_dim(slab, core * half, half, 0)
    part = jnp.where(here, part, jnp.zeros_like(part))
    for bit in bits_of(inner_count)[1:]:
        part = part + swap(part, "inner", bit)
    rest = swap(part, "inner", 1)
    slab_full = jnp.where(
        core == 0,
        jnp.concatenate([part, rest], axis=0),
        jnp.concatenate([rest, part], axis=0),
    )

    gate = halve(term(adjusted_gate), "outer", bits)
    up = halve(term(adjusted_up), "outer", back)
    adjusted = scores(gate, up)
    top = double(adjusted[:half], "outer", bits)
    bottom = double(adjusted[half:], "outer", back)
    full = jnp.zeros((total_tokens, units), jnp.bfloat16)
    for m in range(outer_count):
        for start, blocks in ((0, top), (half, bottom)):
            full = lax.dynamic_update_slice(full, blocks[m], (start, (outer ^ m) * width))
    gram = lax.dot_general(
        slab_full, full, (((0,), (0,)), ((), ())), preferred_element_type=jnp.float32
    )
    return gram / total_tokens


def solution(mesh):
    return jax.shard_map(
        local,
        mesh=mesh,
        in_specs=(
            P(None, "outer"),
            P("outer", "inner"),
            P("outer", "inner"),
            P("outer", "inner"),
            P("outer", "inner"),
            P(),
        ),
        out_specs=P("outer", "inner"),
        check_vma=False,
    )
```

time: 550 us -> 226 us (0.41)
  waiting for transfers between devices: 415 us -> 103 us
  starting transfers between devices: 0.3 us -> 46.9 us
  blocking collectives: 30.5 us -> 0 us
  other arithmetic: 30.2 us -> 17.6 us
  between operations: 13.3 us -> 1.07 us
  matrix products: 56.5 us -> 49.6 us
    reduce_scatter x1 -> x0, waiting for transfers between devices: 258 us -> none  [local(): lax.psum_scatter(jnp.concatenate(parts, axis=1), 'outer', scatter_dimensi...]
    ppermute x0 -> x23, waiting for transfers between devices: none -> 103 us  [swap(): return lax.ppermute(value, axis, [(i, i ^ bit) for i in range(size)])]
    all_gather x2 -> x0, waiting for transfers between devices: 99.2 us -> none  [the longest x1 50.1 us: local(): lax.all_gather(slab, 'outer', axis=0, tiled=True)]
    psum x1 -> x0, waiting for transfers between devices: 57.3 us -> none  [spread(): return lax.psum(kept, axis)]
    ppermute x0 -> x23, starting transfers between devices: none -> 46.9 us  [swap(): return lax.ppermute(value, axis, [(i, i ^ bit) for i in range(size)])]
    psum x2 -> x0, blocking collectives: 30.5 us -> none  [the longest x1 15.4 us: local(): sums = lax.psum(jnp.sum(hidden, axis=0, keepdims=True), 'outer')]
    concatenate x1, other arithmetic: 20.5 us -> 1.35 us  [local(): jnp.concatenate([halve(lambda b: slab_term(b)[:half], 'outer', bits), hal...]
    dot_general x5 -> x9, matrix products: 56.5 us -> 49.6 us  [the longest x8 42.9 us: block(): jnp.dot(tokens, part, preferred_element_type=jnp.float32).astype(WIRE)]
  transfers between devices with their start and end apart: 4 -> 23, of which waited for: 4 -> 9; matrix products, arithmetic and copies ran while one was open for 0% -> 24% of each run, Pallas kernels for 0% -> 0%
where the time goes in v1:
time: 226 us; the launch traced here: 224 us
  waiting for transfers between devices  103 us (46%)
  matrix products  49.6 us (22%)
  starting transfers between devices  46.9 us (21%)
  other arithmetic  17.6 us (8%)
  local copies, waits for them, and re-layouts  5.41 us (2%)
    ppermute x23, waiting for transfers between devices, swap(): return lax.ppermute(value, axis, [(i, i ^ bit) for i in range(size)])  103 us
    ppermute x23, starting transfers between devices, swap(): return lax.ppermute(value, axis, [(i, i ^ bit) for i in range(size)])  46.9 us
    dot_general x8, matrix products, block(): jnp.dot(tokens, part, preferred_element_type=jnp.float32).astype(WIRE)  42.9 us
    dot_general x1, matrix products, local(): lax.dot_general(slab_full, full, (((0,), (0,)), ((), ())), preferred_elem...  6.76 us
    select_n x1, other arithmetic, local(): other = jnp.where(core == 0, slab_up, slab_gate)  5.09 us
    reduce_sum x2, other arithmetic, scores(): mean = jnp.mean(hidden, axis=0, keepdims=True)  4.84 us
    add x1, other arithmetic, local(): mine = mine + swap(other, 'inner', 1)  4.7 us
  transfers between devices with their start and end apart: 23, of which 9 were waited for; matrix products, arithmetic and copies ran while one was open for 24% of the time, Pallas kernels for 0%

profile of v1, /device:TPU:0, one launch (start us, length us, event | category | flops | bytes accessed | tf_op | source)
XLA Modules:
  0.0 223.7 jit_solution(7353474988620205060)
XLA Ops:
  0.7 4.3 %conditional.1 = (f16[512,3584]{1,0:T(8,128)(2,1)}, f16[512,3584]{1,0:T(8,128)(2,1)}) conditional(s32[]{:T(128)} %convert_element_type.139, () %tuple.13, (bf16[512,2048]{1,0:T(8,128)(2,1)}, bf16[2048,3584]{1,0:T(8,128)(2,1)}, bf16[2048,3584]{1,0:T(8,128)(2,1)}) %tuple.14), branch_computations={%region_0.0_spmd, %region_1.0_spmd} | conditional | flops 15036055552 | bytes 108003400 | solution.py:75
  0.7 2.1 broadcast.47
  2.7 2.2 broadcast.47.clone
  4.9 5.1 %broadcast_select_fusion = f16[512,3584]{1,0:T(8,128)(2,1)} fusion(f16[512,3584]{1,0:T(8,128)(2,1)} %get-tuple-element.17, f16[512,3584]{1,0:T(8,128)(2,1)} %get-tuple-element.16, pred[]{:T(512)S(6)} %eq.8), kind=kLoop, calls=%fused_computation.20 | loop fusion | flops 1835008 | bytes 11010049 | tf_op jit(solution)/shard_map/jit(_where)/select_n | solution.py:80
  10.5 5.3 %fusion.51 = f16[512,896]{1,0:T(8,128)(2,1)} fusion(bf16[512,2048]{1,0:T(8,128)(2,1)S(1)} %copy-done.3, bf16[2048,3584]{1,0:T(8,128)(2,1)} %param.11, s32[]{:T(128)S(6)} %select_n.98), kind=kOutput, calls=%fused_computation.45 | convolution fusion | flops 1879506944 | bytes 6684676 | tf_op jit(solution)/shard_map/dot_general | solution.py:63
  15.8 2.5 %collective-permute-start.12 = (f16[512,896]{1,0:T(8,128)(2,1)}, f16[512,896]{1,0:T(8,128)(2,1)}, u32[]{:S(2)}, u32[]{:S(2)}) collective-permute-start(f16[512,896]{1,0:T(8,128)(2,1)} %fusion.51), channel_id=1, source_target_pairs={{0,8},{8,0},{16,24},{24,16},{1,9},{9,1},{17,25},{25,17},{2,10},{10... | collective-permute-start | bytes 2752520 | tf_op jit(solution)/shard_map/ppermute | solution.py:11
  18.3 5.3 %fusion.45 = f16[512,896]{1,0:T(8,128)(2,1)} fusion(bf16[512,2048]{1,0:T(8,128)(2,1)S(1)} %copy-done.3, bf16[2048,3584]{1,0:T(8,128)(2,1)} %param.12, s32[]{:T(128)S(6)} %select_n.98), kind=kOutput, calls=%fused_computation.43 | convolution fusion | flops 1879506944 | bytes 6684676 | tf_op jit(solution)/shard_map/dot_general | solution.py:63
  25.1 5.3 %fusion.54 = f16[512,896]{1,0:T(8,128)(2,1)} fusion(bf16[512,2048]{1,0:T(8,128)(2,1)S(1)} %copy-done.3, bf16[2048,3584]{1,0:T(8,128)(2,1)} %param.11, s32[]{:T(128)S(6)} %select_n.96), kind=kOutput, calls=%fused_computation.46 | convolution fusion | flops 1879506944 | bytes 6684676 | tf_op jit(solution)/shard_map/dot_general | solution.py:63
  30.9 4.7 %select_add_fusion = f16[512,3584]{1,0:T(8,128)(2,1)S(1)} fusion(f16[512,3584]{1,0:T(8,128)(2,1)} %collective-permute-done, f16[512,3584]{1,0:T(8,128)(2,1)} %get-tuple-element.16, f16[512,3584]{1,0:T(8,128)(2,1)} %get-tuple-element.17, pred[]{:T(512)S(6)} %eq.8), kind=kLoop, calls=%fused_computation.19 | loop fusion | flops 3670016 | bytes 14680065 | tf_op jit(solution)/shard_map/add | solution.py:81
  37.6 5.3 %fusion.48 = f16[512,896]{1,0:T(8,128)(2,1)} fusion(bf16[512,2048]{1,0:T(8,128)(2,1)S(1)} %copy-done.3, bf16[2048,3584]{1,0:T(8,128)(2,1)} %param.12, s32[]{:T(128)S(6)} %select_n.97), kind=kOutput, calls=%fused_computation.44 | convolution fusion | flops 1879506944 | bytes 6684676 | tf_op jit(solution)/shard_map/dot_general | solution.py:63
  43.4 25.7 %collective-permute-done.2 = f16[256,896]{1,0:T(8,128)(2,1)S(1)} collective-permute-done((f16[256,896]{1,0:T(8,128)(2,1)S(1)}, f16[256,896]{1,0:T(8,128)(2,1)S(1)}, u32[]{:S(2)}, u32[]{:S(2)}) %collective-permute-start.2) | collective-permute-done | bytes 458784 | tf_op jit(solution)/shard_map/ppermute | solution.py:11
  71.4 5.6 %fusion.19 = f16[512,896]{1,0:T(8,128)(2,1)} fusion(f16[512,896]{1,0:T(8,128)(2,1)} %collective-permute-done.12, bf16[512,2048]{1,0:T(8,128)(2,1)S(1)} %copy-done.3, bf16[2048,3584]{1,0:T(8,128)(2,1)} %param.11, s32[]{:T(128)S(6)} %select_n.97), kind=kOutput, calls=%fused_computation.28 | convolution fusion | flops 1881341952 | bytes 7602180 | tf_op jit(solution)/shard_map/dot_general | solution.py:63
  84.6 7.8 %collective-permute-done.3 = f16[256,896]{1,0:T(8,128)(2,1)S(1)} collective-permute-done((f16[256,896]{1,0:T(8,128)(2,1)S(1)}, f16[256,896]{1,0:T(8,128)(2,1)S(1)}, u32[]{:S(2)}, u32[]{:S(2)}) %collective-permute-start.3) | collective-permute-done | bytes 458784 | tf_op jit(solution)/shard_map/ppermute | solution.py:11
  96.3 5.6 %fusion.16 = f16[512,896]{1,0:T(8,128)(2,1)} fusion(f16[512,896]{1,0:T(8,128)(2,1)} %collective-permute-done.15, bf16[512,2048]{1,0:T(8,128)(2,1)S(1)} %copy-done.4, bf16[2048,3584]{1,0:T(8,128)(2,1)} %param.12, s32[]{:T(128)S(6)} %select_n.96), kind=kOutput, calls=%fused_computation.23 | convolution fusion | flops 1881341952 | bytes 7602180 | tf_op jit(solution)/shard_map/dot_general | solution.py:63
  101.9 38.4 %collective-permute-done.4 = f16[256,896]{1,0:T(8,128)(2,1)S(1)} collective-permute-done((f16[256,896]{1,0:T(8,128)(2,1)S(1)}, f16[256,896]{1,0:T(8,128)(2,1)S(1)}, u32[]{:S(2)}, u32[]{:S(2)}) %collective-permute-start.4) | collective-permute-done | bytes 458784 | tf_op jit(solution)/shard_map/ppermute | solution.py:11
  143.4 5.4 %fusion.21 = f16[896,512]{0,1:T(8,128)(2,1)} fusion(bf16[512,2048]{1,0:T(8,128)(2,1)S(1)} %copy-done.4, bf16[2048,3584]{1,0:T(8,128)(2,1)} %param.11, s32[]{:T(128)S(6)} %select_n.95), kind=kOutput, calls=%fused_computation.35 | convolution fusion | flops 1879506944 | bytes 6684676 | tf_op jit(solution)/shard_map/dot_general | solution.py:63
  149.0 5.1 %fusion.33 = f16[896,512]{0,1:T(8,128)(2,1)S(1)} fusion(bf16[512,2048]{1,0:T(8,128)(2,1)} %param.8, bf16[2048,3584]{1,0:T(8,128)(2,1)} %param.12, s32[]{:T(128)S(6)} %select_n.95), kind=kOutput, calls=%fused_computation.39 | convolution fusion | flops 1879506944 | bytes 6684676 | tf_op jit(solution)/shard_map/dot_general | solution.py:63
  154.1 7.7 %collective-permute-done.16 = f16[512,896]{1,0:T(8,128)(2,1)} collective-permute-done((f16[512,896]{1,0:T(8,128)(2,1)}, f16[512,896]{1,0:T(8,128)(2,1)}, u32[]{:S(2)}, u32[]{:S(2)}) %collective-permute-start.16) | collective-permute-done | bytes 917536 | tf_op jit(solution)/shard_map/ppermute | solution.py:11
  161.8 2.8 %fusion.79 = (f32[896]{0:T(1024)S(1)}, f32[512,896]{1,0:T(8,128)S(1)}) fusion(f16[512,896]{1,0:T(8,128)(2,1)} %collective-permute-done.16, f16[512,896]{1,0:T(8,128)(2,1)} %collective-permute-done.14, f16[896,512]{0,1:T(8,128)(2,1)S(1)} %fusion.33, f16[512,896]{1,0:T(8,128)(2,1)} %collective-permute-done.13, f16[512,896]{1,0:T(8,128)(2,1)S(1)} %collective-permute-done.11, ...), kind=kLoop, calls=%fused_computation.86 | loop fusion | flops 7339136 | bytes 7343616 | tf_op jit(solution)/shard_map/reduce_sum | solution.py:43
  164.8 2.1 fusion.78
  173.1 4.5 %collective-permute-done.8 = bf16[256,896]{1,0:T(8,128)(2,1)S(1)} collective-permute-done((bf16[256,896]{1,0:T(8,128)(2,1)S(1)}, bf16[256,896]{1,0:T(8,128)(2,1)S(1)}, u32[]{:S(2)}, u32[]{:S(2)}) %collective-permute-start.8) | collective-permute-done | bytes 458784 | tf_op jit(solution)/shard_map/ppermute | solution.py:11
  177.8 20.4 %collective-permute-start.9 = (bf16[256,896]{1,0:T(8,128)(2,1)S(1)}, bf16[256,896]{1,0:T(8,128)(2,1)S(1)}, u32[]{:S(2)}, u32[]{:S(2)}) collective-permute-start(bf16[256,896]{1,0:T(8,128)(2,1)S(1)} %fusion.95), channel_id=1, source_target_pairs={{0,4},{1,5},{2,6},{3,7},{4,0},{5,1},{6,2},{7,3},{8,12},{9,13},{10,... | collective-permute-start | bytes 1376264 | tf_op jit(solution)/shard_map/ppermute | solution.py:11
  201.4 13.5 %collective-permute-done.9 = bf16[256,896]{1,0:T(8,128)(2,1)S(1)} collective-permute-done((bf16[256,896]{1,0:T(8,128)(2,1)S(1)}, bf16[256,896]{1,0:T(8,128)(2,1)S(1)}, u32[]{:S(2)}, u32[]{:S(2)}) %collective-permute-start.9) | collective-permute-done | bytes 458784 | tf_op jit(solution)/shard_map/ppermute | solution.py:11
  216.9 6.8 %convolution_multiply_fusion = f32[896,3584]{1,0:T(8,128)} fusion(bf16[512,3584]{1,0:T(8,128)(2,1)S(1)} %constant_dynamic-update-slice_fusion.4, bf16[256,896]{1,0:T(8,128)(2,1)S(1)} %collective-permute-done.10, bf16[256,896]{1,0:T(8,128)(2,1)S(1)} %add.125, pred[]{:T(512)S(6)} %eq.8), kind=kOutput, calls=%fused_computation.2 | convolution fusion | flops 3295674368 | bytes 17432576 | tf_op jit(solution)/shard_map/dot_general | solution.py:119
  (70 shorter events, 33.6 us)
Async XLA Ops:
  10.0 20.9 %collective-permute-start = (f16[512,3584]{1,0:T(8,128)(2,1)}, f16[512,3584]{1,0:T(8,128)(2,1)}, u32[]{:S(2)}, u32[]{:S(2)}) collective-permute-start(f16[512,3584]{1,0:T(8,128)(2,1)} %broadcast_select_fusion), channel_id=1, source_target_pairs={{0,1},{1,0},{2,3},{3,2},{4,5},{5,4},{6,7},{7,6},{8,9},{9,8},{10,11... | collective-permute-start | bytes 11010056 | tf_op jit(solution)/shard_map/ppermute | solution.py:11
  15.8 55.5 %collective-permute-start.12 = (f16[512,896]{1,0:T(8,128)(2,1)}, f16[512,896]{1,0:T(8,128)(2,1)}, u32[]{:S(2)}, u32[]{:S(2)}) collective-permute-start(f16[512,896]{1,0:T(8,128)(2,1)} %fusion.51), channel_id=1, source_target_pairs={{0,8},{8,0},{16,24},{24,16},{1,9},{9,1},{17,25},{25,17},{2,10},{10... | collective-permute-start | bytes 2752520 | tf_op jit(solution)/shard_map/ppermute | solution.py:11
  23.6 71.2 %collective-permute-start.15 = (f16[512,896]{1,0:T(8,128)(2,1)}, f16[512,896]{1,0:T(8,128)(2,1)}, u32[]{:S(2)}, u32[]{:S(2)}) collective-permute-start(f16[512,896]{1,0:T(8,128)(2,1)} %fusion.45), channel_id=1, source_target_pairs={{0,16},{8,24},{16,0},{24,8},{1,17},{9,25},{17,1},{25,9},{2,18},{10... | collective-permute-start | bytes 2752520 | tf_op jit(solution)/shard_map/ppermute | solution.py:11
  30.4 123.7 %collective-permute-start.11 = (f16[512,896]{1,0:T(8,128)(2,1)}, f16[512,896]{1,0:T(8,128)(2,1)S(1)}, u32[]{:S(2)}, u32[]{:S(2)}) collective-permute-start(f16[512,896]{1,0:T(8,128)(2,1)} %fusion.54), channel_id=1, source_target_pairs={{0,8},{8,0},{16,24},{24,16},{1,9},{9,1},{17,25},{25,17},{2,10},{10... | collective-permute-start | bytes 2752520 | tf_op jit(solution)/shard_map/ppermute | solution.py:11
  36.0 33.1 %collective-permute-start.2 = (f16[256,896]{1,0:T(8,128)(2,1)S(1)}, f16[256,896]{1,0:T(8,128)(2,1)S(1)}, u32[]{:S(2)}, u32[]{:S(2)}) collective-permute-start(f16[256,896]{1,0:T(8,128)(2,1)S(1)} %get-tuple-element.31), channel_id=1, source_target_pairs={{0,8},{8,0},{16,24},{24,16},{1,9},{9,1},{17,25},{25,17},{2,10},{10... | collective-permute-start | bytes 1376264 | tf_op jit(solution)/shard_map/ppermute | solution.py:11
  42.9 35.9 %collective-permute-start.1 = (f16[256,896]{1,0:T(8,128)(2,1)S(1)}, f16[256,896]{1,0:T(8,128)(2,1)S(1)}, u32[]{:S(2)}, u32[]{:S(2)}) collective-permute-start(f16[256,896]{1,0:T(8,128)(2,1)S(1)} %get-tuple-element.30), channel_id=1, source_target_pairs={{0,8},{8,0},{16,24},{24,16},{1,9},{9,1},{17,25},{25,17},{2,10},{10... | collective-permute-start | bytes 1376264 | tf_op jit(solution)/shard_map/ppermute | solution.py:11
  69.2 13.4 %collective-permute-start.5 = (f16[256,896]{1,0:T(8,128)(2,1)S(1)}, f16[256,896]{1,0:T(8,128)(2,1)S(1)}, u32[]{:S(2)}, u32[]{:S(2)}) collective-permute-start(f16[256,896]{1,0:T(8,128)(2,1)S(1)} %get-tuple-element.32), channel_id=1, source_target_pairs={{0,16},{8,24},{16,0},{24,8},{1,17},{9,25},{17,1},{25,9},{2,18},{10... | collective-permute-start | bytes 1376264 | tf_op jit(solution)/shard_map/ppermute | solution.py:11
  71.3 21.1 %collective-permute-start.3 = (f16[256,896]{1,0:T(8,128)(2,1)S(1)}, f16[256,896]{1,0:T(8,128)(2,1)S(1)}, u32[]{:S(2)}, u32[]{:S(2)}) collective-permute-start(f16[256,896]{1,0:T(8,128)(2,1)S(1)} %add_convert_fusion.1), channel_id=1, source_target_pairs={{0,16},{8,24},{16,0},{24,8},{1,17},{9,25},{17,1},{25,9},{2,18},{10... | collective-permute-start | bytes 1376264 | tf_op jit(solution)/shard_map/ppermute | solution.py:11
  77.0 19.3 %copy-start.4 = (bf16[512,2048]{1,0:T(8,128)(2,1)S(1)}, bf16[512,2048]{1,0:T(8,128)(2,1)}, u32[]{:S(2)}) copy-start(bf16[512,2048]{1,0:T(8,128)(2,1)} %param.8) | copy-start | bytes 6291460
  78.8 75.2 %collective-permute-start.14 = (f16[512,896]{1,0:T(8,128)(2,1)}, f16[512,896]{1,0:T(8,128)(2,1)}, u32[]{:S(2)}, u32[]{:S(2)}) collective-permute-start(f16[512,896]{1,0:T(8,128)(2,1)} %fusion.48), channel_id=1, source_target_pairs={{0,16},{8,24},{16,0},{24,8},{1,17},{9,25},{17,1},{25,9},{2,18},{10... | collective-permute-start | bytes 2752520 | tf_op jit(solution)/shard_map/ppermute | solution.py:11
  82.6 71.5 %collective-permute-start.13 = (f16[512,896]{1,0:T(8,128)(2,1)}, f16[512,896]{1,0:T(8,128)(2,1)}, u32[]{:S(2)}, u32[]{:S(2)}) collective-permute-start(f16[512,896]{1,0:T(8,128)(2,1)} %fusion.19), channel_id=1, source_target_pairs={{0,16},{8,24},{16,0},{24,8},{1,17},{9,25},{17,1},{25,9},{2,18},{10... | collective-permute-start | bytes 2752520 | tf_op jit(solution)/shard_map/ppermute | solution.py:11
  92.4 47.9 %collective-permute-start.4 = (f16[256,896]{1,0:T(8,128)(2,1)S(1)}, f16[256,896]{1,0:T(8,128)(2,1)S(1)}, u32[]{:S(2)}, u32[]{:S(2)}) collective-permute-start(f16[256,896]{1,0:T(8,128)(2,1)S(1)} %get-tuple-element.33), channel_id=1, source_target_pairs={{0,16},{8,24},{16,0},{24,8},{1,17},{9,25},{17,1},{25,9},{2,18},{10... | collective-permute-start | bytes 1376264 | tf_op jit(solution)/shard_map/ppermute | solution.py:11
  94.8 47.1 %collective-permute-start.6 = (f16[256,896]{1,0:T(8,128)(2,1)S(1)}, f16[256,896]{1,0:T(8,128)(2,1)S(1)}, u32[]{:S(2)}, u32[]{:S(2)}) collective-permute-start(f16[256,896]{1,0:T(8,128)(2,1)S(1)} %get-tuple-element.29), channel_id=1, source_target_pairs={{0,8},{8,0},{16,24},{24,16},{1,9},{9,1},{17,25},{25,17},{2,10},{10... | collective-permute-start | bytes 1376264 | tf_op jit(solution)/shard_map/ppermute | solution.py:11
  140.3 21.4 %collective-permute-start.16 = (f16[512,896]{1,0:T(8,128)(2,1)}, f16[512,896]{1,0:T(8,128)(2,1)}, u32[]{:S(2)}, u32[]{:S(2)}) collective-permute-start(f16[512,896]{1,0:T(8,128)(2,1)} %fusion.16), channel_id=1, source_target_pairs={{0,8},{8,0},{16,24},{24,16},{1,9},{9,1},{17,25},{25,17},{2,10},{10... | collective-permute-start | bytes 2752520 | tf_op jit(solution)/shard_map/ppermute | solution.py:11
  143.4 21.4 %collective-permute-start.7 = (f32[512,896]{1,0:T(8,128)}, f32[512,896]{1,0:T(8,128)}, u32[]{:S(2)}, u32[]{:S(2)}) collective-permute-start(f32[512,896]{1,0:T(8,128)} %pad_maximum_fusion), channel_id=1, source_target_pairs={{0,1},{1,0},{2,3},{3,2},{4,5},{5,4},{6,7},{7,6},{8,9},{9,8},{10,11... | collective-permute-start | bytes 5505032 | tf_op jit(solution)/shard_map/ppermute | solution.py:11
  167.2 10.4 %collective-permute-start.8 = (bf16[256,896]{1,0:T(8,128)(2,1)S(1)}, bf16[256,896]{1,0:T(8,128)(2,1)S(1)}, u32[]{:S(2)}, u32[]{:S(2)}) collective-permute-start(bf16[256,896]{1,0:T(8,128)(2,1)S(1)} %fusion.68), channel_id=1, source_target_pairs={{0,2},{1,3},{2,0},{3,1},{4,6},{5,7},{6,4},{7,5},{8,10},{9,11},{10,... | collective-permute-start | bytes 1376264 | tf_op jit(solution)/shard_map/ppermute | solution.py:11
  169.0 29.2 %collective-permute-start.17 = (bf16[256,896]{1,0:T(8,128)(2,1)S(1)}, bf16[256,896]{1,0:T(8,128)(2,1)S(1)}, u32[]{:S(2)}, u32[]{:S(2)}) collective-permute-start(bf16[256,896]{1,0:T(8,128)(2,1)S(1)} %get-tuple-element.36), channel_id=1, source_target_pairs={{0,8},{8,0},{16,24},{24,16},{1,9},{9,1},{17,25},{25,17},{2,10},{10... | collective-permute-start | bytes 1376264 | tf_op jit(solution)/shard_map/ppermute | solution.py:11
  170.6 44.6 %collective-permute-start.19 = (bf16[256,896]{1,0:T(8,128)(2,1)S(1)}, bf16[256,896]{1,0:T(8,128)(2,1)S(1)}, u32[]{:S(2)}, u32[]{:S(2)}) collective-permute-start(bf16[256,896]{1,0:T(8,128)(2,1)S(1)} %get-tuple-element.36), channel_id=1, source_target_pairs={{0,16},{8,24},{16,0},{24,8},{1,17},{9,25},{17,1},{25,9},{2,18},{10... | collective-permute-start | bytes 1376264 | tf_op jit(solution)/shard_map/ppermute | solution.py:11
  172.1 29.2 %collective-permute-start.18 = (bf16[256,896]{1,0:T(8,128)(2,1)S(1)}, bf16[256,896]{1,0:T(8,128)(2,1)S(1)}, u32[]{:S(2)}, u32[]{:S(2)}) collective-permute-start(bf16[256,896]{1,0:T(8,128)(2,1)S(1)} %get-tuple-element.34), channel_id=1, source_target_pairs={{0,8},{8,0},{16,24},{24,16},{1,9},{9,1},{17,25},{25,17},{2,10},{10... | collective-permute-start | bytes 1376264 | tf_op jit(solution)/shard_map/ppermute | solution.py:11
  172.6 27.2 %collective-permute-start.20 = (bf16[256,896]{1,0:T(8,128)(2,1)S(1)}, bf16[256,896]{1,0:T(8,128)(2,1)S(1)}, u32[]{:S(2)}, u32[]{:S(2)}) collective-permute-start(bf16[256,896]{1,0:T(8,128)(2,1)S(1)} %get-tuple-element.34), channel_id=1, source_target_pairs={{0,16},{8,24},{16,0},{24,8},{1,17},{9,25},{17,1},{25,9},{2,18},{10... | collective-permute-start | bytes 1376264 | tf_op jit(solution)/shard_map/ppermute | solution.py:11
  177.8 37.2 %collective-permute-start.9 = (bf16[256,896]{1,0:T(8,128)(2,1)S(1)}, bf16[256,896]{1,0:T(8,128)(2,1)S(1)}, u32[]{:S(2)}, u32[]{:S(2)}) collective-permute-start(bf16[256,896]{1,0:T(8,128)(2,1)S(1)} %fusion.95), channel_id=1, source_target_pairs={{0,4},{1,5},{2,6},{3,7},{4,0},{5,1},{6,2},{7,3},{8,12},{9,13},{10,... | collective-permute-start | bytes 1376264 | tf_op jit(solution)/shard_map/ppermute | solution.py:11
  198.2 17.1 %collective-permute-start.21 = (bf16[256,896]{1,0:T(8,128)(2,1)S(1)}, bf16[256,896]{1,0:T(8,128)(2,1)S(1)}, u32[]{:S(2)}, u32[]{:S(2)}) collective-permute-start(bf16[256,896]{1,0:T(8,128)(2,1)S(1)} %collective-permute-done.17), channel_id=1, source_target_pairs={{0,16},{8,24},{16,0},{24,8},{1,17},{9,25},{17,1},{25,9},{2,18},{10... | collective-permute-start | bytes 1376264 | tf_op jit(solution)/shard_map/ppermute | solution.py:11
  199.8 15.6 %collective-permute-start.22 = (bf16[256,896]{1,0:T(8,128)(2,1)S(1)}, bf16[256,896]{1,0:T(8,128)(2,1)S(1)}, u32[]{:S(2)}, u32[]{:S(2)}) collective-permute-start(bf16[256,896]{1,0:T(8,128)(2,1)S(1)} %collective-permute-done.20), channel_id=1, source_target_pairs={{0,8},{8,0},{16,24},{24,16},{1,9},{9,1},{17,25},{25,17},{2,10},{10... | collective-permute-start | bytes 1376264 | tf_op jit(solution)/shard_map/ppermute | solution.py:11
  215.1 1.9 collective-permute-start.10
  (3 other events, 23.8 us)
